TPU v7x, 128 devices: a whole 4x4x4 slice. The times are simulated.
128 devices in a mesh: fsdp: 8 (over y, z_lo), tensor: 16 (over x, z_hi, core).
Axes of the slice: x: 4, y: 4, z: 4 (z_hi: 2, z_lo: 2; z = z_hi * 2 + z_lo), core: 2. Of those that a mesh axis runs over, the one named last changes fastest.
Arguments:
- tokens: bfloat16 [16384, 1024], P(('fsdp', 'tensor')), may hold values from -6 to 6
- cotangent: bfloat16 [16384, 1024], P(('fsdp', 'tensor')), may hold values from -6 to 6
- w_qkv: bfloat16 [2, 1024, 16, 192], P(None, 'fsdp', 'tensor'), may hold values from -0.1875 to 0.1875
- qv_bias: bfloat16 [2, 16, 128], P(None, 'tensor'), may hold values from -3 to 3
- w_out: bfloat16 [2, 16, 64, 1024], P(None, 'tensor', None, 'fsdp'), may hold values from -0.75 to 0.75
- w_fc1: bfloat16 [2, 1024, 4096], P(None, 'fsdp', 'tensor'), may hold values from -0.1875 to 0.1875
- fc1_bias: bfloat16 [2, 4096], P(None, 'tensor'), may hold values from -3 to 3
- w_fc2: bfloat16 [2, 4096, 1024], P(None, 'tensor', 'fsdp'), may hold values from -0.09375 to 0.09375
- norm_gain: bfloat16 [2, 2, 1024], P(None, None, 'fsdp'), may hold values from 0.25 to 1.75
- norm_bias: bfloat16 [2, 2, 1024], P(None, None, 'fsdp'), may hold values from -2 to 2
- layer_scale: bfloat16 [2, 2, 1024], P(None, None, 'fsdp'), may hold values from 0.5 to 1.5
- out_bias: bfloat16 [2, 2, 1024], P(None, None, 'fsdp'), may hold values from -2 to 2
Outputs:
- out_tokens: bfloat16 [16384, 1024], P(('fsdp', 'tensor'))
- grad_tokens: float32 [16384, 1024], P(('fsdp', 'tensor'))
- grad_w_qkv: float32 [2, 1024, 16, 192], P(None, 'fsdp', 'tensor')
- grad_qv_bias: float32 [2, 16, 128], P(None, 'tensor')
- grad_w_out: float32 [2, 16, 64, 1024], P(None, 'tensor', None, 'fsdp')
- grad_w_fc1: float32 [2, 1024, 4096], P(None, 'fsdp', 'tensor')
- grad_fc1_bias: float32 [2, 4096], P(None, 'tensor')
- grad_w_fc2: float32 [2, 4096, 1024], P(None, 'tensor', 'fsdp')
- grad_norm_gain: float32 [2, 2, 1024], P(None, None, 'fsdp')
- grad_norm_bias: float32 [2, 2, 1024], P(None, None, 'fsdp')
- grad_layer_scale: float32 [2, 2, 1024], P(None, None, 'fsdp')
- grad_out_bias: float32 [2, 2, 1024], P(None, None, 'fsdp')
All inputs are finite; a program needn't handle non-finite values.
Results may differ from a plain program's by a relative error of at most 0.02.
Values may be sent and summed in bfloat16 or wider, within the bound.
A program may use at most 192 MiB of HBM per device.

v0:
```python
import jax
import jax.numpy as jnp
from jax import lax
from jax.experimental import pallas as pl
from jax.experimental.pallas import tpu as pltpu
from jax.sharding import Mesh
from jax.sharding import PartitionSpec as P

D = 1024
HD = 64
SEQ = 1024
ROWS = 128
NX = 4
NF = 8
NZ = 2
F32 = jnp.float32
BF = jnp.bfloat16
TENSOR = ("tensor_0", "tensor_1", "tensor_2")
FSDP_TENSOR = ("fsdp", "tensor_0", "tensor_1", "tensor_2")
MESH = pl.DeviceIdType.MESH
EPS = 1e-06
ROOT_HALF = 0.7071067811865476
INV_ROOT_TAU = 0.3989422804014327
HALF = ROWS // 2
TOP = pl.ds(0, HALF)
BOTTOM = pl.ds(HALF, HALF)
VMEM_BYTES = 60 * 1024 * 1024
OWN, LEFT, RIGHT, FAR = 0, 1, 2, 3


def dot_nn(left, right):
    return lax.dot_general(left, right, (((1,), (0,)), ((), ())), preferred_element_type=F32)


def dot_nt(left, right):
    return lax.dot_general(left, right, (((1,), (1,)), ((), ())), preferred_element_type=F32)


def dot_tn(left, right):
    return lax.dot_general(left, right, (((0,), (0,)), ((), ())), preferred_element_type=F32)


def norm_parts(stream):
    centre = stream - jnp.mean(stream, axis=-1, keepdims=True)
    inverse = lax.rsqrt(jnp.mean(centre * centre, axis=-1, keepdims=True) + EPS)
    return centre * inverse, inverse


def norm_backward(grad_out, normal, inverse, gain):
    scaled = grad_out * gain
    return inverse * (
        scaled
        - jnp.mean(scaled, axis=-1, keepdims=True)
        - normal * jnp.mean(scaled * normal, axis=-1, keepdims=True)
    )


def group_index():
    return lax.axis_index("fsdp"), lax.axis_index("tensor_1")


def group_peer(step):
    f, z = group_index()
    at = lax.rem(f * NZ + z + step, NF * NZ)
    return at // NZ, lax.rem(at, NZ)


def group_id(step):
    f, z = group_peer(step)
    return {"fsdp": f, "tensor_1": z}


def cols(f, width=128):
    return pl.ds(pl.multiple_of(f * width, width), width)


VIEWS = {
    "qkv": lambda ref, f, z: ref.at[:, z, :, cols(f)],
    "out": lambda ref, f, z: ref.at[z, :, cols(f)],
    "small": lambda ref, f, z: ref.at[z, :, :, cols(f)],
    "fc1": lambda ref, f, z: ref.at[cols(f), cols(z, 256)],
    "fc2": lambda ref, f, z: ref.at[cols(z, 256), cols(f)],
    "vec": lambda ref, f, z: ref.at[:, cols(f)],
    "unit": lambda ref, f, z: ref.at[z],
}


def each_peer(act):
    def step(s, _):
        act(s)
        return 0

    lax.fori_loop(1, NF * NZ, step, 0)


class Gather:
    def __init__(self, kind, src, dst, send, recv):
        self.view, self.src, self.dst = VIEWS[kind], src, dst
        self.send, self.recv = send, recv

    def copy(self, step):
        return pltpu.make_async_remote_copy(
            src_ref=self.src,
            dst_ref=self.view(self.dst, *group_index()),
            send_sem=self.send.at[step],
            recv_sem=self.recv.at[step],
            device_id=group_id(step),
            device_id_type=MESH,
        )

    def local(self):
        return pltpu.make_async_copy(
            self.src, self.view(self.dst, *group_index()), self.send.at[0]
        )

    def start(self):
        self.local().start()
        each_peer(lambda s: self.copy(s).start())

    def wait(self):
        self.local().wait()
        each_peer(lambda s: self.copy(s).wait())


class Scatter:
    def __init__(self, kind, src, land, send, recv):
        self.view, self.src, self.land = VIEWS[kind], src, land
        self.send, self.recv = send, recv

    def copy(self, step):
        return pltpu.make_async_remote_copy(
            src_ref=self.view(self.src, *group_peer(step)),
            dst_ref=self.land.at[step],
            send_sem=self.send.at[step],
            recv_sem=self.recv.at[step],
            device_id=group_id(step),
            device_id_type=MESH,
        )

    def local(self):
        return pltpu.make_async_copy(
            self.view(self.src, *group_index()), self.land.at[0], self.send.at[0]
        )

    def start(self):
        self.local().start()
        each_peer(lambda s: self.copy(s).start())

    def total(self):
        self.local().wait()
        each_peer(lambda s: self.copy(s).wait())
        return sum(self.land[s].astype(F32) for s in range(NF * NZ))


class Swap:
    def __init__(self, src, dst, send, recv):
        x, z = lax.axis_index("tensor_0"), lax.axis_index("tensor_1")
        self.moves = lax.rem(x // 2 + z, 2) == 1
        self.remote = pltpu.make_async_remote_copy(
            src_ref=src,
            dst_ref=dst,
            send_sem=send,
            recv_sem=recv,
            device_id=swap_id(),
            device_id_type=MESH,
        )
        self.stay = pltpu.make_async_copy(src, dst, send)

    def start(self):
        pl.when(self.moves)(self.remote.start)
        pl.when(jnp.logical_not(self.moves))(self.stay.start)

    def wait(self):
        pl.when(self.moves)(self.remote.wait)
        pl.when(jnp.logical_not(self.moves))(self.stay.wait)


def swap_id():
    x, z = lax.axis_index("tensor_0"), lax.axis_index("tensor_1")
    return {"tensor_0": lax.rem(x + 2, NX), "tensor_1": 1 - z}


def ring_id(step):
    x, c = lax.axis_index("tensor_0"), lax.axis_index("tensor_2")
    at = lax.rem(x * 2 + c + step, 2 * NX)
    return {"tensor_0": at // 2, "tensor_2": lax.rem(at, 2)}


def greet():
    barrier = pltpu.get_barrier_semaphore()

    def signal(where):
        pl.semaphore_signal(barrier, inc=1, device_id=where, device_id_type=MESH)

    for s in range(1, 2 * NX):
        signal(ring_id(s))
    signal(swap_id())
    each_peer(lambda s: signal(group_id(s)))
    return lambda: pl.semaphore_wait(barrier, 2 * NX + NF * NZ - 1)


class Ring:
    def __init__(self, part, pin, sout, rin, held, gsend, grecv, ssend, srecv):
        self.x, self.c = lax.axis_index("tensor_0"), lax.axis_index("tensor_2")
        self.at = [self.x] + [lax.rem(self.x + s, NX) for s in (3, 1, 2)]
        self.part, self.pin = part, pin
        self.sout, self.rin, self.held = sout, rin, held
        self.gsend, self.grecv, self.ssend, self.srecv = gsend, grecv, ssend, srecv
        self.left = {"tensor_0": self.at[LEFT]}
        self.right = {"tensor_0": self.at[RIGHT]}
        self.twin = {"tensor_2": 1 - self.c}

    def gcopy(self, i):
        who, rows, to = (
            (OWN, None, self.twin),
            (OWN, TOP, self.right),
            (OWN, BOTTOM, self.right),
            (OWN, BOTTOM, self.left),
            (OWN, TOP, self.left),
            (LEFT, TOP, self.right),
            (RIGHT, BOTTOM, self.left),
            (LEFT, None, self.twin),
            (RIGHT, None, self.twin),
            (FAR, TOP, self.twin),
            (FAR, BOTTOM, self.twin),
        )[i]
        ref = self.gath.at[self.at[who], self.c]
        if rows is not None:
            ref = ref.at[rows]
        return pltpu.make_async_remote_copy(
            src_ref=ref,
            dst_ref=ref,
            send_sem=self.gsend.at[i],
            recv_sem=self.grecv.at[i],
            device_id=to,
            device_id_type=MESH,
        )

    def set_own(self, gath, rows):
        self.gath = gath
        self.gath[self.x, self.c] = rows
        for i in (1, 3, 2, 4, 0):
            self.gcopy(i).start()

    def arrive(self, who):
        def got(i):
            self.gcopy(i).wait_recv()

        def go(i):
            self.gcopy(i).start()

        if who == OWN:
            got(0)
        elif who == LEFT:
            got(1), go(5), got(3), go(6), got(2), go(7), got(4), go(8), got(7)
        elif who == RIGHT:
            got(8)
        else:
            got(5), go(9), got(6), go(10), got(9), got(10)

    def rows(self, who):
        return self.gath[self.at[who]].reshape(2 * ROWS, D)

    def pcopy(self, who):
        return pltpu.make_async_remote_copy(
            src_ref=self.part.at[who, 1 - self.c],
            dst_ref=self.pin.at[who],
            send_sem=self.ssend.at[6 + who],
            recv_sem=self.srecv.at[6 + who],
            device_id=self.twin,
            device_id_type=MESH,
        )

    def scopy(self, i):
        return pltpu.make_async_remote_copy(
            src_ref=self.sout.at[i],
            dst_ref=self.rin.at[i],
            send_sem=self.ssend.at[i],
            recv_sem=self.srecv.at[i],
            device_id=self.left if i in (1, 4, 5) else self.right,
            device_id_type=MESH,
        )

    def put(self, who, value):
        self.part[who] = value.astype(BF).reshape(2, ROWS, D)
        self.pcopy(who).start()

    def send(self, i, value):
        self.sout[i] = value.astype(BF)
        self.scopy(i).start()

    def flush(self, who):
        self.pcopy(who).wait_recv()
        total = self.part[who, self.c].astype(F32) + self.pin[who].astype(F32)
        if who == FAR:
            self.send(0, total[:HALF])
            self.send(1, total[HALF:])
        elif who == RIGHT:
            self.send(2, total[HALF:])
            self.held[0] = total[:HALF]
        elif who == LEFT:
            self.send(4, total[:HALF])
            self.held[1] = total[HALF:]

    def merge(self):
        self.scopy(0).wait_recv()
        self.send(3, self.held[0] + self.rin[0].astype(F32))
        self.scopy(1).wait_recv()
        self.send(5, self.held[1] + self.rin[1].astype(F32))

    def finish(self):
        self.pcopy(OWN).wait_recv()
        total = self.part[OWN, self.c].astype(F32) + self.pin[OWN].astype(F32)
        for i in (2, 4, 3, 5):
            self.scopy(i).wait_recv()
        top = total[:HALF] + self.rin[3].astype(F32) + self.rin[4].astype(F32)
        bottom = total[HALF:] + self.rin[2].astype(F32) + self.rin[5].astype(F32)
        return jnp.concatenate([top, bottom], axis=0)

    def drain(self):
        for i in range(11):
            self.gcopy(i).wait_send()
        for i in range(6):
            self.scopy(i).wait_send()
        for i in range(4):
            self.pcopy(i).wait_send()


RING_SCRATCH = [
    pltpu.VMEM((NX, 2, ROWS, D), BF),
    pltpu.VMEM((NX, ROWS, D), BF),
    pltpu.VMEM((6, HALF, D), BF),
    pltpu.VMEM((6, HALF, D), BF),
    pltpu.VMEM((2, HALF, D), F32),
    pltpu.SemaphoreType.DMA((11,)),
    pltpu.SemaphoreType.DMA((11,)),
    pltpu.SemaphoreType.DMA((10,)),
    pltpu.SemaphoreType.DMA((10,)),
]

def lane_head(shape):
    return lax.broadcasted_iota(jnp.int32, shape, len(shape) - 1) // HD


def row_sum(value):
    return jnp.sum(value, axis=0, keepdims=True)


PIECE = {
    "qkv": (3, HD, 128),
    "out": (HD, 128),
    "fc1": (128, 256),
    "fc2": (256, 128),
    "vec": (16, 128),
    "unit": (8, 128),
}
HEADS = (NX, 2 * ROWS, 128)


def sems(*shape):
    return [pltpu.SemaphoreType.DMA(shape)] * 2


SCRATCH = dict(
    small_src=pltpu.VMEM((2, 16, 128), F32),
    small=pltpu.VMEM((NZ, 2, 16, D), F32),
    qkv_src=pltpu.VMEM((2, 3, HD, 128), BF),
    wqkv=pltpu.VMEM((2, 3, NZ, HD, D), BF),
    wout=pltpu.VMEM((2, NZ, HD, D), BF),
    wfc1=pltpu.VMEM((2, D, 512), BF),
    wfc2=pltpu.VMEM((2, 512, D), BF),
    start=pltpu.VMEM((ROWS, D), BF),
    first_grad=pltpu.VMEM((ROWS, D), BF),
    ending=pltpu.VMEM((ROWS, D), BF),
    stream=pltpu.VMEM((3, ROWS, D), F32),
    mid=pltpu.VMEM((2, ROWS, D), F32),
    branch=pltpu.VMEM((2, 2, ROWS, D), F32),
    grad=pltpu.VMEM((ROWS, D), F32),
    normed=pltpu.VMEM((2, 2, NX, 2, ROWS, D), BF),
    q=pltpu.VMEM((2, *HEADS), BF),
    k=pltpu.VMEM((2, *HEADS), BF),
    v=pltpu.VMEM((2, *HEADS), BF),
    mixed=pltpu.VMEM((2, *HEADS), BF),
    lse=pltpu.VMEM((2, NX, 2, 1, 2 * ROWS), F32),
    hidden=pltpu.VMEM((2, NX, 2 * ROWS, 512), BF),
    slope=pltpu.VMEM((2, NX, 2 * ROWS, 512), BF),
    mk=pltpu.VMEM((2, *HEADS), BF),
    mv=pltpu.VMEM((2, *HEADS), BF),
    turned=pltpu.VMEM((NX, 128, 2 * ROWS), BF),
    mixt=pltpu.VMEM((128, 2 * ROWS), F32),
    gath=pltpu.VMEM((2, NX, 2, ROWS, D), BF),
    pre=pltpu.VMEM((NX, 2 * ROWS, 512), BF),
    gmix=pltpu.VMEM(HEADS, BF),
    dq=pltpu.VMEM(HEADS, BF),
    dk=pltpu.VMEM((SEQ, 128), F32),
    dv=pltpu.VMEM((SEQ, 128), F32),
    dall=pltpu.VMEM((NX, 2 * ROWS, 384), BF),
    sums=pltpu.VMEM((2, 2, 8, D), F32),
    dqkv=pltpu.VMEM((3, NZ, HD, D), BF),
    dout=pltpu.VMEM((NZ, HD, D), BF),
    dfc1=pltpu.VMEM((D, 512), BF),
    dfc2=pltpu.VMEM((512, D), BF),
    vec_src=pltpu.VMEM((16, D), F32),
    unit_src=pltpu.VMEM((NZ, 8, 128), F32),
    vec_sum=pltpu.VMEM((16, 128), F32),
    land_qkv=pltpu.VMEM((2, NF * NZ, *PIECE["qkv"]), BF),
    land_out=pltpu.VMEM((2, NF * NZ, *PIECE["out"]), BF),
    land_fc1=pltpu.VMEM((2, NF * NZ, *PIECE["fc1"]), BF),
    land_fc2=pltpu.VMEM((2, NF * NZ, *PIECE["fc2"]), BF),
    land_vec=pltpu.VMEM((NF * NZ, *PIECE["vec"]), F32),
    land_unit=pltpu.VMEM((NF * NZ, *PIECE["unit"]), F32),
    land_ring=pltpu.VMEM((2 * NX, *PIECE["vec"]), F32),
    small_sems=sems(NF * NZ),
    qkv_sems=sems(2, NF * NZ),
    out_sems=sems(2, NF * NZ),
    fc1_sems=sems(2, NF * NZ),
    fc2_sems=sems(2, NF * NZ),
    dqkv_sems=sems(2, NF * NZ),
    dout_sems=sems(2, NF * NZ),
    dfc1_sems=sems(2, NF * NZ),
    dfc2_sems=sems(2, NF * NZ),
    vec_sems=sems(NF * NZ),
    unit_sems=sems(NF * NZ),
    swap_sems=sems(4),
    ring_sems=sems(2 * NX),
    ring=RING_SCRATCH,
)


def scratch_list():
    flat = []
    for item in SCRATCH.values():
        flat += item if isinstance(item, list) else [item]
    return flat


class Refs:
    def __init__(self, flat):
        flat = list(flat)
        for name, item in SCRATCH.items():
            if isinstance(item, list):
                setattr(self, name, [flat.pop(0) for _ in item])
            else:
                setattr(self, name, flat.pop(0))


IN = ("tokens", "cotangent", "w_qkv", "qv_bias", "w_out", "w_fc1", "fc1_bias", "w_fc2")
IN += ("norm_gain", "norm_bias", "layer_scale", "out_bias")
OUT = ("out_tokens", "grad_tokens", "g_qkv", "g_out", "g_fc1", "g_fc2", "g_vec", "g_unit")


def pair(send_recv, *at):
    return [s.at[at] for s in send_recv]


class Program:
    def __init__(self, flat):
        for name, ref in zip(IN + OUT, flat):
            setattr(self, name, ref)
        self.r = Refs(flat[len(IN + OUT) :])
        self.ring = Ring(*self.r.ring)

    def small_job(self):
        r = self.r
        return Gather("small", r.small_src, r.small, *r.small_sems)

    def head_jobs(self, l):
        r = self.r
        return (
            Gather("qkv", r.qkv_src.at[l], r.wqkv.at[l], *pair(r.qkv_sems, l)),
            Gather("out", self.w_out.at[l], r.wout.at[l], *pair(r.out_sems, l)),
        )

    def unit_jobs(self, l):
        r = self.r
        return (
            Gather("fc1", self.w_fc1.at[l], r.wfc1.at[l], *pair(r.fc1_sems, l)),
            Gather("fc2", self.w_fc2.at[l], r.wfc2.at[l], *pair(r.fc2_sems, l)),
        )

    def head_sums(self, l):
        r = self.r
        return (
            Scatter("qkv", r.dqkv, r.land_qkv.at[l], *pair(r.dqkv_sems, l)),
            Scatter("out", r.dout, r.land_out.at[l], *pair(r.dout_sems, l)),
        )

    def unit_sums(self, l):
        r = self.r
        return (
            Scatter("fc1", r.dfc1, r.land_fc1.at[l], *pair(r.dfc1_sems, l)),
            Scatter("fc2", r.dfc2, r.land_fc2.at[l], *pair(r.dfc2_sems, l)),
        )

    def finish_heads(self, l):
        qkv, out = self.head_sums(l)
        self.g_qkv[l] = qkv.total().reshape(3 * HD, 128).T
        self.g_out[l] = out.total()

    def finish_units(self, l):
        fc1, fc2 = self.unit_sums(l)
        self.g_fc1[l] = fc1.total()
        self.g_fc2[l] = fc2.total()

    def swap(self, i, src, dst):
        return Swap(src, dst, *pair(self.r.swap_sems, i))

    def run(self):
        r = self.r
        greeted = greet()
        for l in range(2):
            at = 0
            for ref in (self.norm_gain, self.norm_bias, self.layer_scale, self.out_bias):
                r.small_src[l, at : at + 2, :] = ref[l].astype(F32)
                at += 2
            bias = self.fc1_bias[...].astype(F32)[l : l + 1]
            r.small_src[l, 8:9, :] = bias[:, :128]
            r.small_src[l, 9:10, :] = bias[:, 128:]
            r.small_src[l, 10:11, :] = self.qv_bias[...].astype(F32)[l : l + 1]
            r.small_src[l, 11:16, :] = jnp.zeros((5, 128), F32)
            turned = self.w_qkv[l].astype(F32).T.astype(BF)
            r.qkv_src[l] = turned.reshape(3, HD, 128)
        greeted()
        tokens = self.swap(0, self.tokens, r.start)
        cotangent = self.swap(1, self.cotangent, r.first_grad)
        tokens.start()
        self.small_job().start()
        for job in self.head_jobs(0):
            job.start()
        cotangent.start()
        tokens.wait()
        r.stream[0] = r.start[...].astype(F32)
        self.small_job().wait()
        lax.fori_loop(0, 2, self.forward, 0)
        r.ending[...] = r.stream[2].astype(BF)
        ending = self.swap(2, r.ending, self.out_tokens)
        ending.start()
        cotangent.wait()
        r.grad[...] = r.first_grad[...].astype(F32)
        lax.fori_loop(0, 2, self.backward, 0)
        back = self.swap(3, r.grad, self.grad_tokens)
        back.start()
        self.last_sums()
        ending.wait()
        back.wait()

    def forward(self, l, _):
        self.attn_forward(l)
        self.mlp_forward(l)
        return 0

    def backward(self, i, _):
        self.mlp_backward(1 - i)
        self.attn_backward(1 - i)
        return 0

    def attn_forward(self, l):
        r, ring = self.r, self.ring
        vec = r.small[0, l]
        normal, _ = norm_parts(r.stream[l])
        ring.set_own(r.normed.at[l, 0], (normal * vec[0:1] + vec[2:3]).astype(BF))
        bias_a, bias_b = r.small[0, l][10:11, 0:128], r.small[1, l][10:11, 0:128]
        shift = jnp.concatenate(
            [
                bias_a[:, :HD],
                bias_b[:, :HD],
                jnp.zeros((1, 128), F32),
                bias_a[:, HD:],
                bias_b[:, HD:],
            ],
            axis=1,
        )
        for job in self.head_jobs(l):
            job.wait()
        for job in self.unit_jobs(l):
            job.start()
        weights = r.wqkv[l].reshape(3 * 2 * HD, D)
        for who in (OWN, LEFT, RIGHT, FAR):
            ring.arrive(who)
            at = ring.at[who]
            qkv = (dot_nt(ring.rows(who), weights) + shift).astype(BF)
            keys, values = qkv[:, 128:256], qkv[:, 256:]
            r.q[l, at] = qkv[:, :128] * 0.125
            r.k[l, at] = keys
            r.v[l, at] = values
            head = lane_head((2 * ROWS, 128))
            for h in range(2):
                r.mk[h, at] = jnp.where(head == h, keys, jnp.zeros_like(keys))
            r.turned[at] = values.astype(F32).T.astype(BF)
        for who in (FAR, LEFT, RIGHT, OWN):
            at = ring.at[who]

            def head_step(h, _, at=at):
                scores = dot_nt(r.mk[h].reshape(SEQ, 128), r.q[l, at])
                highest = jnp.max(scores, axis=0, keepdims=True)
                weights = jnp.exp(scores - highest)
                total = jnp.sum(weights, axis=0, keepdims=True)
                probs = (weights * (1.0 / total)).astype(BF)
                span = pl.ds(pl.multiple_of(h * HD, HD), HD)
                mixed = jnp.zeros((HD, 2 * ROWS), F32)
                for part in range(NX):
                    mixed = mixed + dot_nn(
                        r.turned[part, span, :],
                        probs[part * 2 * ROWS : (part + 1) * 2 * ROWS],
                    )
                r.mixt[span, :] = mixed
                r.lse[l, at, h] = highest + jnp.log(total)
                return 0

            lax.fori_loop(0, 2, head_step, 0)
            mixed = r.mixt[...].T.astype(BF)
            r.mixed[l, at] = mixed
            ring.put(who, dot_nn(mixed, r.wout[l].reshape(2 * HD, D)))
            if who == LEFT:
                ring.flush(FAR)
            elif who == RIGHT:
                ring.flush(LEFT)
                ring.flush(RIGHT)
                ring.merge()
        branch = ring.finish() + vec[6:7]
        r.branch[l, 0] = branch
        r.mid[l] = r.stream[l] + vec[4:5] * branch
        ring.drain()

    def mlp_forward(self, l):
        r, ring = self.r, self.ring
        vec = r.small[0, l]
        normal, _ = norm_parts(r.mid[l])
        ring.set_own(r.normed.at[l, 1], (normal * vec[1:2] + vec[3:4]).astype(BF))
        bias = jnp.concatenate(
            [r.small[z, l][row : row + 1, 0:128] for z in range(NZ) for row in (8, 9)], axis=1
        )
        for job in self.unit_jobs(l):
            job.wait()

        @pl.when(l == 0)
        def _():
            for job in self.head_jobs(1):
                job.start()

        for who in (OWN, LEFT, RIGHT, FAR):
            ring.arrive(who)
            at = ring.at[who]
            pre = dot_nn(ring.rows(who), r.wfc1[l]) + bias
            phi = 0.5 * (1.0 + lax.erf(pre * ROOT_HALF))
            hidden = (pre * phi).astype(BF)
            slope = phi + pre * INV_ROOT_TAU * jnp.exp(-0.5 * pre * pre)
            r.slope[l, at] = slope.astype(BF)
            r.hidden[l, at] = hidden
            ring.put(who, dot_nn(hidden, r.wfc2[l]))
            if who == RIGHT:
                ring.flush(LEFT)
                ring.flush(RIGHT)
        ring.flush(FAR)
        ring.merge()
        branch = ring.finish() + vec[7:8]
        r.branch[l, 1] = branch
        r.stream[l + 1] = r.mid[l] + vec[5:6] * branch
        ring.drain()

    def begin_backward(self, l, i, gath):
        r = self.r
        g = r.grad[...]
        scaled = r.small[0, l][4 + i : 5 + i] * g
        self.ring.set_own(gath, scaled.astype(BF))
        r.sums[l, i] = jnp.zeros((8, D), F32)
        r.sums[l, i, 2:3, :] = row_sum(r.branch[l, i] * g)
        r.sums[l, i, 3:4, :] = row_sum(scaled)

    def end_backward(self, l, i, stream):
        r = self.r
        back = self.ring.finish()
        normal, inverse = norm_parts(stream)
        r.sums[l, i, 0:1, :] = row_sum(back * normal)
        r.sums[l, i, 1:2, :] = row_sum(back)
        gain = r.small[0, l][i : i + 1]
        r.grad[...] += norm_backward(back, normal, inverse, gain)
        self.ring.drain()

    def mlp_backward(self, l):
        r, ring = self.r, self.ring
        gath = r.gath.at[0]
        self.begin_backward(l, 1, gath)
        unit = jnp.zeros((1, 512), F32)
        for who in (OWN, LEFT, RIGHT, FAR):
            ring.arrive(who)
            at = ring.at[who]
            back = dot_nt(ring.rows(who), r.wfc2[l]) * r.slope[l, at].astype(F32)
            back = back.astype(BF)
            r.pre[at] = back
            unit = unit + row_sum(back.astype(F32))
            ring.put(who, dot_nt(back, r.wfc1[l]))
            if who == RIGHT:
                ring.flush(LEFT)
                ring.flush(RIGHT)
        ring.flush(FAR)
        r.sums[l, 1, 4:5, 0:512] = unit
        fc1, fc2 = self.unit_sums(l)
        r.dfc2[...] = dot_tn(
            r.hidden[l].reshape(SEQ, 512), gath[...].reshape(SEQ, D)
        ).astype(BF)
        fc2.start()
        ring.merge()
        r.dfc1[...] = dot_tn(
            r.normed[l, 1].reshape(SEQ, D), r.pre[...].reshape(SEQ, 512)
        ).astype(BF)
        fc1.start()

        @pl.when(l == 0)
        def _():
            self.finish_heads(1)

        self.end_backward(l, 1, r.mid[l])

    def attn_backward(self, l):
        r, ring = self.r, self.ring
        gath = r.gath.at[1]
        self.begin_backward(l, 0, gath)
        head = lane_head((2 * ROWS, 128))
        for part in range(NX):
            keys, values = r.k[l, part], r.v[l, part]
            for h in range(2):
                r.mk[h, part] = jnp.where(head == h, keys, jnp.zeros_like(keys))
                r.mv[h, part] = jnp.where(head == h, values, jnp.zeros_like(values))
            r.turned[part] = keys.astype(F32).T.astype(BF)
        r.dk[...] = jnp.zeros((SEQ, 128), F32)
        r.dv[...] = jnp.zeros((SEQ, 128), F32)
        for who in (OWN, LEFT, RIGHT, FAR):
            ring.arrive(who)
            at = ring.at[who]
            r.gmix[at] = dot_nt(ring.rows(who), r.wout[l].reshape(2 * HD, D)).astype(BF)

            def head_step(h, _, at=at):
                queries, mine = r.q[l, at], r.gmix[at]
                probs = jnp.exp(dot_nt(r.mk[h].reshape(SEQ, 128), queries) - r.lse[l, at, h])
                back = dot_nt(r.mv[h].reshape(SEQ, 128), mine)
                delta = jnp.sum(probs * back, axis=0, keepdims=True)
                dscores = (probs * (back - delta)).astype(BF)
                span = pl.ds(pl.multiple_of(h * HD, HD), HD)
                turned = jnp.zeros((HD, 2 * ROWS), F32)
                for part in range(NX):
                    turned = turned + dot_nn(
                        r.turned[part, span, :],
                        dscores[part * 2 * ROWS : (part + 1) * 2 * ROWS],
                    )
                r.mixt[span, :] = turned * 0.125
                mask = head == h
                r.dk[...] += dot_nn(dscores, jnp.where(mask, queries, jnp.zeros_like(queries)))
                r.dv[...] += dot_nn(
                    probs.astype(BF), jnp.where(mask, mine, jnp.zeros_like(mine))
                )
                return 0

            lax.fori_loop(0, 2, head_step, 0)
            r.dq[at] = r.mixt[...].T.astype(BF)
        for part in range(NX):
            span = slice(part * 2 * ROWS, (part + 1) * 2 * ROWS)
            r.dall[part] = jnp.concatenate(
                [r.dq[part], r.dk[span, :].astype(BF), r.dv[span, :].astype(BF)], axis=1
            )
        weights = r.wqkv[l].reshape(3 * 2 * HD, D)
        for who in (FAR, LEFT, RIGHT, OWN):
            ring.put(who, dot_nn(r.dall[ring.at[who]], weights))
            if who == LEFT:
                ring.flush(FAR)
            elif who == RIGHT:
                ring.flush(LEFT)
                ring.flush(RIGHT)
        qkv, out = self.head_sums(l)
        whole = r.dall[...].reshape(SEQ, 384)
        dqkv = dot_tn(whole, r.normed[l, 0].reshape(SEQ, D)).astype(BF)
        r.dqkv[...] = dqkv.reshape(3, NZ, HD, D)
        qkv.start()
        ring.merge()
        dout = dot_tn(r.mixed[l].reshape(SEQ, 128), gath[...].reshape(SEQ, D)).astype(BF)
        r.dout[...] = dout.reshape(NZ, HD, D)
        out.start()
        unit = row_sum(whole.astype(F32))
        r.sums[l, 0, 4:5, 0:256] = jnp.concatenate(
            [
                unit[:, 0:HD],
                unit[:, 256 : 256 + HD],
                unit[:, HD:128],
                unit[:, 256 + HD : 384],
            ],
            axis=1,
        )
        self.finish_units(l)
        self.end_backward(l, 0, r.stream[l])

    def last_sums(self):
        r = self.r
        for l in range(2):
            for i in range(2):
                sums = r.sums[l, i]
                for kind in range(4):
                    row = kind * 4 + l * 2 + i
                    r.vec_src[row : row + 1, :] = sums[kind : kind + 1]
            heads, units = r.sums[l, 0], r.sums[l, 1]
            for z in range(NZ):
                for at, row in ((0, l * 2), (128, l * 2 + 1)):
                    at = at + z * 256
                    r.unit_src[z, row : row + 1, :] = units[4:5, at : at + 128]
                r.unit_src[z, 4 + l : 5 + l, :] = heads[4:5, z * 128 : (z + 1) * 128]
                r.unit_src[z, 6 + l : 7 + l, :] = jnp.zeros((1, 128), F32)
        vec = Scatter("vec", r.vec_src, r.land_vec, *r.vec_sems)
        unit = Scatter("unit", r.unit_src, r.land_unit, *r.unit_sems)
        vec.start()
        unit.start()
        r.vec_sum[...] = vec.total()

        def copy(step):
            return pltpu.make_async_remote_copy(
                src_ref=r.vec_sum,
                dst_ref=r.land_ring.at[step],
                send_sem=r.ring_sems[0].at[step],
                recv_sem=r.ring_sems[1].at[step],
                device_id=ring_id(step),
                device_id_type=MESH,
            )

        for s in range(1, 2 * NX):
            copy(s).start()
        self.g_unit[...] = unit.total()
        self.finish_heads(0)
        total = r.vec_sum[...]
        for s in range(1, 2 * NX):
            copy(s).wait()
            total = total + r.land_ring[s]
        self.g_vec[...] = total


def whole_kernel(*flat):
    Program(flat).run()


def run_whole(*args):
    outs = [
        jax.ShapeDtypeStruct((ROWS, D), BF),
        jax.ShapeDtypeStruct((ROWS, D), F32),
        jax.ShapeDtypeStruct((2, 128, 3 * HD), F32),
        jax.ShapeDtypeStruct((2, HD, 128), F32),
        jax.ShapeDtypeStruct((2, 128, 256), F32),
        jax.ShapeDtypeStruct((2, 256, 128), F32),
        jax.ShapeDtypeStruct((16, 128), F32),
        jax.ShapeDtypeStruct((8, 128), F32),
    ]
    whole = pl.BlockSpec(memory_space=pltpu.VMEM)
    return pl.pallas_call(
        whole_kernel,
        out_shape=outs,
        in_specs=[whole] * len(args),
        out_specs=[whole] * len(outs),
        scratch_shapes=scratch_list(),
        compiler_params=pltpu.CompilerParams(
            collective_id=0, has_side_effects=True, vmem_limit_bytes=VMEM_BYTES
        ),
        cost_estimate=pl.CostEstimate(
            flops=24_000_000_000, bytes_accessed=8_000_000, transcendentals=10_000_000
        ),
    )(*args)


def on_device(
    tokens,
    cotangent,
    w_qkv,
    qv_bias,
    w_out,
    w_fc1,
    fc1_bias,
    w_fc2,
    norm_gain,
    norm_bias,
    layer_scale,
    out_bias,
):
    out_tokens, grad_tokens, g_qkv, g_out, g_fc1, g_fc2, g_vec, g_unit = run_whole(
        tokens,
        cotangent,
        w_qkv.reshape(2, 128, 3 * HD),
        qv_bias.reshape(2, 128),
        w_out.reshape(2, HD, 128),
        w_fc1,
        fc1_bias,
        w_fc2,
        norm_gain,
        norm_bias,
        layer_scale,
        out_bias,
    )
    vec = g_vec.reshape(4, 2, 2, 128)
    return (
        out_tokens,
        grad_tokens,
        g_qkv[:, :, None, :],
        g_unit[4:6][:, None, :],
        g_out[:, None],
        g_fc1,
        g_unit[0:4].reshape(2, 256),
        g_fc2,
        vec[0],
        vec[1],
        vec[2],
        vec[3],
    )


def solution(mesh):
    split = Mesh(
        mesh.devices.reshape(mesh.shape["fsdp"], NX, NZ, 2),
        ("fsdp", "tensor_0", "tensor_1", "tensor_2"),
    )
    return jax.shard_map(
        on_device,
        mesh=split,
        in_specs=(
            P(FSDP_TENSOR, None),
            P(FSDP_TENSOR, None),
            P(None, "fsdp", TENSOR, None),
            P(None, TENSOR, None),
            P(None, TENSOR, None, "fsdp"),
            P(None, "fsdp", TENSOR),
            P(None, TENSOR),
            P(None, TENSOR, "fsdp"),
            P(None, None, "fsdp"),
            P(None, None, "fsdp"),
            P(None, None, "fsdp"),
            P(None, None, "fsdp"),
        ),
        out_specs=(
            P(FSDP_TENSOR, None),
            P(FSDP_TENSOR, None),
            P(None, "fsdp", TENSOR, None),
            P(None, TENSOR, None),
            P(None, TENSOR, None, "fsdp"),
            P(None, "fsdp", TENSOR),
            P(None, TENSOR),
            P(None, TENSOR, "fsdp"),
            P(None, None, "fsdp"),
            P(None, None, "fsdp"),
            P(None, None, "fsdp"),
            P(None, None, "fsdp"),
        ),
        check_vma=False,
    )
```

profile of v0, /device:TPU:1, one launch (start us, length us, event | category | flops | bytes accessed | tf_op | source)
XLA Modules:
  0.0 307.1 jit_solution(16234146723106376807)
XLA Ops:
  0.6 1.7 copy.24
  2.3 294.2 %shard_map.211 = (bf16[128,1024]{1,0:T(8,128)(2,1)}, f32[128,1024]{1,0:T(8,128)}, f32[2,128,192]{2,1,0:T(8,128)}, f32[2,64,128]{2,1,0:T(8,128)}, f32[2,128,256]{...) custom-call(bf16[128,1024]{1,0:T(8,128)(2,1)} %flat_0_.1, bf16[128,1024]{1,0:T(8,128)(2,1)} %flat_1_.1, ...), custom_call_target="tpu_custom_call" | custom-call | flops 24000000000 | bytes 8000000 | tf_op jit(solution)/shard_map/pallas_call | solution.py:849
  296.5 0.0 copy-start
  296.5 1.3 slice.22
  297.8 0.7 slice.23
  298.4 0.6 reshape.48
  299.0 1.4 fusion
  300.4 1.8 copy.25
  302.1 1.7 copy.33
  303.8 0.0 copy-done
  303.8 0.0 copy-start.3
  303.8 0.0 copy-start.2
  303.8 0.8 copy.34
  304.6 0.1 copy-done.3
  304.7 0.6 copy.35
  305.3 0.0 copy-done.2
  305.3 0.0 copy-start.1
  305.3 0.7 copy.36
  306.0 0.3 copy-done.1
  306.4 0.7 copy.37
Async XLA Ops:
  296.5 7.3 %copy-start = (f32[128,1024]{1,0:T(8,128)S(1)}, f32[128,1024]{1,0:T(8,128)}, u32[]{:S(2)}) copy-start(f32[128,1024]{1,0:T(8,128)} %get-tuple-element.57) | copy-start | bytes 1572868
  303.8 0.9 copy-start.3
  303.8 1.5 copy-start.2
  305.3 1.0 copy-start.1
where the time goes:
time: 311 us; the launch traced here: 307 us
  Pallas kernels  294 us (95%)
  local copies, waits for them, and re-layouts  12.2 us (4%)
    pallas_call x1, Pallas kernels, run_whole(): pl.pallas_call(whole_kernel, out_shape=outs, in_specs=[whole] * len(args)...  294 us
    unnamed x15, local copies, waits for them, and re-layouts  8.32 us

commit v1 on v0

--- a/solution.py
+++ b/solution.py
@@ -21,7 +21,11 @@
 EPS = 1e-06
 ROOT_HALF = 0.7071067811865476
 INV_ROOT_TAU = 0.3989422804014327
-HALF = ROWS // 2
+CHUNKS = 2
+PART = ROWS // CHUNKS
+HALF = PART // 2
+GCOPIES = 10
+SCOPIES = 10
 TOP = pl.ds(0, HALF)
 BOTTOM = pl.ds(HALF, HALF)
 VMEM_BYTES = 60 * 1024 * 1024
@@ -210,7 +214,7 @@
         self.right = {"tensor_0": self.at[RIGHT]}
         self.twin = {"tensor_2": 1 - self.c}
 
-    def gcopy(self, i):
+    def gcopy(self, ch, i):
         who, rows, to = (
             (OWN, None, self.twin),
             (OWN, TOP, self.right),
@@ -221,122 +225,203 @@
             (RIGHT, BOTTOM, self.left),
             (LEFT, None, self.twin),
             (RIGHT, None, self.twin),
-            (FAR, TOP, self.twin),
-            (FAR, BOTTOM, self.twin),
+            (FAR, None, self.twin),
         )[i]
-        ref = self.gath.at[self.at[who], self.c]
+        ref = self.gath.at[self.at[who], ch, self.c]
         if rows is not None:
             ref = ref.at[rows]
         return pltpu.make_async_remote_copy(
             src_ref=ref,
             dst_ref=ref,
-            send_sem=self.gsend.at[i],
-            recv_sem=self.grecv.at[i],
+            send_sem=self.gsend.at[ch * GCOPIES + i],
+            recv_sem=self.grecv.at[ch * GCOPIES + i],
             device_id=to,
             device_id_type=MESH,
         )
 
+    def got(self, ch, i):
+        self.gcopy(ch, i).wait_recv()
+
+    def go(self, ch, *which):
+        for i in which:
+            self.gcopy(ch, i).start()
+
     def set_own(self, gath, rows):
         self.gath = gath
-        self.gath[self.x, self.c] = rows
-        for i in (1, 3, 2, 4, 0):
-            self.gcopy(i).start()
-
-    def arrive(self, who):
-        def got(i):
-            self.gcopy(i).wait_recv()
-
-        def go(i):
-            self.gcopy(i).start()
-
-        if who == OWN:
-            got(0)
-        elif who == LEFT:
-            got(1), go(5), got(3), go(6), got(2), go(7), got(4), go(8), got(7)
-        elif who == RIGHT:
-            got(8)
-        else:
-            got(5), go(9), got(6), go(10), got(9), got(10)
+        for ch in range(CHUNKS):
+            gath[self.x, ch, self.c] = rows[ch * PART : (ch + 1) * PART]
+        for ch in range(CHUNKS):
+            self.go(ch, 1, 3, 2, 4, 0)
+
+    def near(self, ch):
+        self.got(ch, 1)
+        self.go(ch, 5)
+        self.got(ch, 3)
+        self.go(ch, 6)
+        self.got(ch, 2)
+        self.go(ch, 7)
+        self.got(ch, 4)
+        self.go(ch, 8)
+
+    def far(self, ch):
+        self.got(ch, 5)
+        self.got(ch, 6)
+        self.go(ch, 9)
+
+    def arrive(self, ch, who):
+        self.got(ch, (0, 7, 8, 9)[who])
+
+    def arrive_both(self, who):
+        self.arrive(0, who)
+        self.arrive(1, who)
+
+    def chunk(self, ch, who):
+        return self.gath[self.at[who], ch].reshape(2 * PART, D)
 
     def rows(self, who):
         return self.gath[self.at[who]].reshape(2 * ROWS, D)
 
-    def pcopy(self, who):
+    def pcopy(self, ch, who):
         return pltpu.make_async_remote_copy(
-            src_ref=self.part.at[who, 1 - self.c],
-            dst_ref=self.pin.at[who],
-            send_sem=self.ssend.at[6 + who],
-            recv_sem=self.srecv.at[6 + who],
+            src_ref=self.part.at[ch, who, 1 - self.c],
+            dst_ref=self.pin.at[ch, who],
+            send_sem=self.ssend.at[ch * SCOPIES + 6 + who],
+            recv_sem=self.srecv.at[ch * SCOPIES + 6 + who],
             device_id=self.twin,
             device_id_type=MESH,
         )
 
-    def scopy(self, i):
+    def scopy(self, ch, i):
         return pltpu.make_async_remote_copy(
-            src_ref=self.sout.at[i],
-            dst_ref=self.rin.at[i],
-            send_sem=self.ssend.at[i],
-            recv_sem=self.srecv.at[i],
+            src_ref=self.sout.at[ch, i],
+            dst_ref=self.rin.at[ch, i],
+            send_sem=self.ssend.at[ch * SCOPIES + i],
+            recv_sem=self.srecv.at[ch * SCOPIES + i],
             device_id=self.left if i in (1, 4, 5) else self.right,
             device_id_type=MESH,
         )
 
-    def put(self, who, value):
-        self.part[who] = value.astype(BF).reshape(2, ROWS, D)
-        self.pcopy(who).start()
-
-    def send(self, i, value):
-        self.sout[i] = value.astype(BF)
-        self.scopy(i).start()
-
-    def flush(self, who):
-        self.pcopy(who).wait_recv()
-        total = self.part[who, self.c].astype(F32) + self.pin[who].astype(F32)
+    def put(self, ch, who, value):
+        self.part[ch, who] = value.astype(BF).reshape(2, PART, D)
+        self.pcopy(ch, who).start()
+
+    def put_both(self, who, value):
+        self.put(0, who, value[: 2 * PART])
+        self.put(1, who, value[2 * PART :])
+
+    def send(self, ch, i, value):
+        self.sout[ch, i] = value.astype(BF)
+        self.scopy(ch, i).start()
+
+    def both_cores(self, ch, who):
+        self.pcopy(ch, who).wait_recv()
+        return self.part[ch, who, self.c].astype(F32) + self.pin[ch, who].astype(F32)
+
+    def flush(self, ch, who):
+        total = self.both_cores(ch, who)
         if who == FAR:
-            self.send(0, total[:HALF])
-            self.send(1, total[HALF:])
+            self.send(ch, 0, total[:HALF])
+            self.send(ch, 1, total[HALF:])
         elif who == RIGHT:
-            self.send(2, total[HALF:])
-            self.held[0] = total[:HALF]
-        elif who == LEFT:
-            self.send(4, total[:HALF])
-            self.held[1] = total[HALF:]
-
-    def merge(self):
-        self.scopy(0).wait_recv()
-        self.send(3, self.held[0] + self.rin[0].astype(F32))
-        self.scopy(1).wait_recv()
-        self.send(5, self.held[1] + self.rin[1].astype(F32))
+            self.send(ch, 2, total[HALF:])
+            self.held[ch, 0] = total[:HALF]
+        else:
+            self.send(ch, 4, total[:HALF])
+            self.held[ch, 1] = total[HALF:]
+
+    def flush_both(self, *which):
+        for who in which:
+            for ch in range(CHUNKS):
+                self.flush(ch, who)
+
+    def merge(self, ch):
+        self.scopy(ch, 0).wait_recv()
+        self.send(ch, 3, self.held[ch, 0] + self.rin[ch, 0].astype(F32))
+        self.scopy(ch, 1).wait_recv()
+        self.send(ch, 5, self.held[ch, 1] + self.rin[ch, 1].astype(F32))
 
     def finish(self):
-        self.pcopy(OWN).wait_recv()
-        total = self.part[OWN, self.c].astype(F32) + self.pin[OWN].astype(F32)
-        for i in (2, 4, 3, 5):
-            self.scopy(i).wait_recv()
-        top = total[:HALF] + self.rin[3].astype(F32) + self.rin[4].astype(F32)
-        bottom = total[HALF:] + self.rin[2].astype(F32) + self.rin[5].astype(F32)
-        return jnp.concatenate([top, bottom], axis=0)
+        rows = []
+        for ch in range(CHUNKS):
+            total = self.both_cores(ch, OWN)
+            for i in (2, 4, 3, 5):
+                self.scopy(ch, i).wait_recv()
+            rin = [self.rin[ch, i].astype(F32) for i in (2, 3, 4, 5)]
+            rows += [total[:HALF] + rin[1] + rin[2], total[HALF:] + rin[0] + rin[3]]
+        return jnp.concatenate(rows, axis=0)
 
     def drain(self):
-        for i in range(11):
-            self.gcopy(i).wait_send()
-        for i in range(6):
-            self.scopy(i).wait_send()
-        for i in range(4):
-            self.pcopy(i).wait_send()
+        for ch in range(CHUNKS):
+            for i in range(GCOPIES):
+                self.gcopy(ch, i).wait_send()
+            for i in range(6):
+                self.scopy(ch, i).wait_send()
+            for i in range(4):
+                self.pcopy(ch, i).wait_send()
+
+    def by_chunks(self, step):
+        self.arrive(0, OWN)
+        step(0, OWN)
+        self.near(0)
+        self.arrive(1, OWN)
+        step(1, OWN)
+        for who in (LEFT, RIGHT):
+            self.arrive(0, who)
+            step(0, who)
+        self.near(1)
+        self.flush(0, LEFT)
+        self.flush(0, RIGHT)
+        self.far(0)
+        self.arrive(1, LEFT)
+        step(1, LEFT)
+        self.arrive(0, FAR)
+        step(0, FAR)
+        self.far(1)
+        self.arrive(1, RIGHT)
+        step(1, RIGHT)
+        self.flush(0, FAR)
+        self.arrive(1, FAR)
+        step(1, FAR)
+        self.flush(1, LEFT)
+        self.flush(1, RIGHT)
+        self.flush(1, FAR)
+        self.merge(0)
+
+    def by_blocks(self, step):
+        self.arrive_both(OWN)
+        step(OWN)
+        self.near(0)
+        self.near(1)
+        self.arrive_both(LEFT)
+        step(LEFT)
+        self.far(0)
+        self.far(1)
+        self.arrive_both(RIGHT)
+        step(RIGHT)
+        self.arrive_both(FAR)
+        step(FAR)
+
+    def back_by_blocks(self, value):
+        for who in (FAR, LEFT, RIGHT, OWN):
+            self.put_both(who, value(who))
+            if who == LEFT:
+                self.flush_both(FAR)
+            elif who == RIGHT:
+                self.flush_both(LEFT, RIGHT)
 
 
 RING_SCRATCH = [
-    pltpu.VMEM((NX, 2, ROWS, D), BF),
-    pltpu.VMEM((NX, ROWS, D), BF),
-    pltpu.VMEM((6, HALF, D), BF),
-    pltpu.VMEM((6, HALF, D), BF),
-    pltpu.VMEM((2, HALF, D), F32),
-    pltpu.SemaphoreType.DMA((11,)),
-    pltpu.SemaphoreType.DMA((11,)),
-    pltpu.SemaphoreType.DMA((10,)),
-    pltpu.SemaphoreType.DMA((10,)),
+    pltpu.VMEM((CHUNKS, NX, 2, PART, D), BF),
+    pltpu.VMEM((CHUNKS, NX, PART, D), BF),
+    pltpu.VMEM((CHUNKS, 6, HALF, D), BF),
+    pltpu.VMEM((CHUNKS, 6, HALF, D), BF),
+    pltpu.VMEM((CHUNKS, 2, HALF, D), F32),
+    pltpu.SemaphoreType.DMA((CHUNKS * GCOPIES,)),
+    pltpu.SemaphoreType.DMA((CHUNKS * GCOPIES,)),
+    pltpu.SemaphoreType.DMA((CHUNKS * SCOPIES,)),
+    pltpu.SemaphoreType.DMA((CHUNKS * SCOPIES,)),
 ]
+
 
 def lane_head(shape):
     return lax.broadcasted_iota(jnp.int32, shape, len(shape) - 1) // HD
@@ -364,7 +449,6 @@
 SCRATCH = dict(
     small_src=pltpu.VMEM((2, 16, 128), F32),
     small=pltpu.VMEM((NZ, 2, 16, D), F32),
-    qkv_src=pltpu.VMEM((2, 3, HD, 128), BF),
     wqkv=pltpu.VMEM((2, 3, NZ, HD, D), BF),
     wout=pltpu.VMEM((2, NZ, HD, D), BF),
     wfc1=pltpu.VMEM((2, D, 512), BF),
@@ -372,11 +456,12 @@
     start=pltpu.VMEM((ROWS, D), BF),
     first_grad=pltpu.VMEM((ROWS, D), BF),
     ending=pltpu.VMEM((ROWS, D), BF),
+    back=pltpu.VMEM((ROWS, D), BF),
     stream=pltpu.VMEM((3, ROWS, D), F32),
     mid=pltpu.VMEM((2, ROWS, D), F32),
     branch=pltpu.VMEM((2, 2, ROWS, D), F32),
     grad=pltpu.VMEM((ROWS, D), F32),
-    normed=pltpu.VMEM((2, 2, NX, 2, ROWS, D), BF),
+    normed=pltpu.VMEM((2, 2, NX, CHUNKS, 2, PART, D), BF),
     q=pltpu.VMEM((2, *HEADS), BF),
     k=pltpu.VMEM((2, *HEADS), BF),
     v=pltpu.VMEM((2, *HEADS), BF),
@@ -388,7 +473,7 @@
     mv=pltpu.VMEM((2, *HEADS), BF),
     turned=pltpu.VMEM((NX, 128, 2 * ROWS), BF),
     mixt=pltpu.VMEM((128, 2 * ROWS), F32),
-    gath=pltpu.VMEM((2, NX, 2, ROWS, D), BF),
+    gath=pltpu.VMEM((2, NX, CHUNKS, 2, PART, D), BF),
     pre=pltpu.VMEM((NX, 2 * ROWS, 512), BF),
     gmix=pltpu.VMEM(HEADS, BF),
     dq=pltpu.VMEM(HEADS, BF),
@@ -446,7 +531,7 @@
 
 IN = ("tokens", "cotangent", "w_qkv", "qv_bias", "w_out", "w_fc1", "fc1_bias", "w_fc2")
 IN += ("norm_gain", "norm_bias", "layer_scale", "out_bias")
-OUT = ("out_tokens", "grad_tokens", "g_qkv", "g_out", "g_fc1", "g_fc2", "g_vec", "g_unit")
+OUT = ("out_tokens", "grad_tokens", "g_qkv", "g_out", "g_fc1", "g_fc2", "g_vec", "g_shift", "g_unit")
 
 
 def pair(send_recv, *at):
@@ -467,7 +552,7 @@
     def head_jobs(self, l):
         r = self.r
         return (
-            Gather("qkv", r.qkv_src.at[l], r.wqkv.at[l], *pair(r.qkv_sems, l)),
+            Gather("qkv", self.w_qkv.at[l], r.wqkv.at[l], *pair(r.qkv_sems, l)),
             Gather("out", self.w_out.at[l], r.wout.at[l], *pair(r.out_sems, l)),
         )
 
@@ -494,7 +579,7 @@
 
     def finish_heads(self, l):
         qkv, out = self.head_sums(l)
-        self.g_qkv[l] = qkv.total().reshape(3 * HD, 128).T
+        self.g_qkv[l] = qkv.total()
         self.g_out[l] = out.total()
 
     def finish_units(self, l):
@@ -518,31 +603,33 @@
             r.small_src[l, 9:10, :] = bias[:, 128:]
             r.small_src[l, 10:11, :] = self.qv_bias[...].astype(F32)[l : l + 1]
             r.small_src[l, 11:16, :] = jnp.zeros((5, 128), F32)
-            turned = self.w_qkv[l].astype(F32).T.astype(BF)
-            r.qkv_src[l] = turned.reshape(3, HD, 128)
         greeted()
         tokens = self.swap(0, self.tokens, r.start)
-        cotangent = self.swap(1, self.cotangent, r.first_grad)
+        self.small_job().start()
         tokens.start()
-        self.small_job().start()
         for job in self.head_jobs(0):
             job.start()
-        cotangent.start()
         tokens.wait()
         r.stream[0] = r.start[...].astype(F32)
         self.small_job().wait()
         lax.fori_loop(0, 2, self.forward, 0)
         r.ending[...] = r.stream[2].astype(BF)
-        ending = self.swap(2, r.ending, self.out_tokens)
-        ending.start()
-        cotangent.wait()
+        self.cotangent_swap().wait()
         r.grad[...] = r.first_grad[...].astype(F32)
         lax.fori_loop(0, 2, self.backward, 0)
-        back = self.swap(3, r.grad, self.grad_tokens)
+        r.start[...] = r.grad[...].astype(BF)
+        back = self.swap(3, r.start, r.back)
         back.start()
         self.last_sums()
-        ending.wait()
+        self.ending_swap().wait()
         back.wait()
+        self.grad_tokens[...] = r.back[...].astype(F32)
+
+    def cotangent_swap(self):
+        return self.swap(1, self.cotangent, self.r.first_grad)
+
+    def ending_swap(self):
+        return self.swap(2, self.r.ending, self.out_tokens)
 
     def forward(self, l, _):
         self.attn_forward(l)
@@ -575,8 +662,8 @@
         for job in self.unit_jobs(l):
             job.start()
         weights = r.wqkv[l].reshape(3 * 2 * HD, D)
-        for who in (OWN, LEFT, RIGHT, FAR):
-            ring.arrive(who)
+
+        def project(who):
             at = ring.at[who]
             qkv = (dot_nt(ring.rows(who), weights) + shift).astype(BF)
             keys, values = qkv[:, 128:256], qkv[:, 256:]
@@ -587,10 +674,14 @@
             for h in range(2):
                 r.mk[h, at] = jnp.where(head == h, keys, jnp.zeros_like(keys))
             r.turned[at] = values.astype(F32).T.astype(BF)
-        for who in (FAR, LEFT, RIGHT, OWN):
+
+        ring.by_blocks(project)
+        pl.when(l == 0)(self.cotangent_swap().start)
+
+        def attend(who):
             at = ring.at[who]
 
-            def head_step(h, _, at=at):
+            def head_step(h, _):
                 scores = dot_nt(r.mk[h].reshape(SEQ, 128), r.q[l, at])
                 highest = jnp.max(scores, axis=0, keepdims=True)
                 weights = jnp.exp(scores - highest)
@@ -610,13 +701,11 @@
             lax.fori_loop(0, 2, head_step, 0)
             mixed = r.mixt[...].T.astype(BF)
             r.mixed[l, at] = mixed
-            ring.put(who, dot_nn(mixed, r.wout[l].reshape(2 * HD, D)))
-            if who == LEFT:
-                ring.flush(FAR)
-            elif who == RIGHT:
-                ring.flush(LEFT)
-                ring.flush(RIGHT)
-                ring.merge()
+            return dot_nn(mixed, r.wout[l].reshape(2 * HD, D))
+
+        ring.back_by_blocks(attend)
+        ring.merge(0)
+        ring.merge(1)
         branch = ring.finish() + vec[6:7]
         r.branch[l, 0] = branch
         r.mid[l] = r.stream[l] + vec[4:5] * branch
@@ -638,21 +727,19 @@
             for job in self.head_jobs(1):
                 job.start()
 
-        for who in (OWN, LEFT, RIGHT, FAR):
-            ring.arrive(who)
+        def step(ch, who):
             at = ring.at[who]
-            pre = dot_nn(ring.rows(who), r.wfc1[l]) + bias
+            span = slice(ch * 2 * PART, (ch + 1) * 2 * PART)
+            pre = dot_nn(ring.chunk(ch, who), r.wfc1[l]) + bias
             phi = 0.5 * (1.0 + lax.erf(pre * ROOT_HALF))
             hidden = (pre * phi).astype(BF)
             slope = phi + pre * INV_ROOT_TAU * jnp.exp(-0.5 * pre * pre)
-            r.slope[l, at] = slope.astype(BF)
-            r.hidden[l, at] = hidden
-            ring.put(who, dot_nn(hidden, r.wfc2[l]))
-            if who == RIGHT:
-                ring.flush(LEFT)
-                ring.flush(RIGHT)
-        ring.flush(FAR)
-        ring.merge()
+            r.slope[l, at, span, :] = slope.astype(BF)
+            r.hidden[l, at, span, :] = hidden
+            ring.put(ch, who, dot_nn(hidden, r.wfc2[l]))
+
+        ring.by_chunks(step)
+        ring.merge(1)
         branch = ring.finish() + vec[7:8]
         r.branch[l, 1] = branch
         r.stream[l + 1] = r.mid[l] + vec[5:6] * branch
@@ -681,30 +768,27 @@
         r, ring = self.r, self.ring
         gath = r.gath.at[0]
         self.begin_backward(l, 1, gath)
-        unit = jnp.zeros((1, 512), F32)
-        for who in (OWN, LEFT, RIGHT, FAR):
-            ring.arrive(who)
+
+        def step(ch, who):
             at = ring.at[who]
-            back = dot_nt(ring.rows(who), r.wfc2[l]) * r.slope[l, at].astype(F32)
+            span = slice(ch * 2 * PART, (ch + 1) * 2 * PART)
+            back = dot_nt(ring.chunk(ch, who), r.wfc2[l]) * r.slope[l, at, span, :].astype(F32)
             back = back.astype(BF)
-            r.pre[at] = back
-            unit = unit + row_sum(back.astype(F32))
-            ring.put(who, dot_nt(back, r.wfc1[l]))
-            if who == RIGHT:
-                ring.flush(LEFT)
-                ring.flush(RIGHT)
-        ring.flush(FAR)
-        r.sums[l, 1, 4:5, 0:512] = unit
+            r.pre[at, span, :] = back
+            ring.put(ch, who, dot_nt(back, r.wfc1[l]))
+
+        ring.by_chunks(step)
         fc1, fc2 = self.unit_sums(l)
         r.dfc2[...] = dot_tn(
             r.hidden[l].reshape(SEQ, 512), gath[...].reshape(SEQ, D)
         ).astype(BF)
         fc2.start()
-        ring.merge()
+        ring.merge(1)
         r.dfc1[...] = dot_tn(
             r.normed[l, 1].reshape(SEQ, D), r.pre[...].reshape(SEQ, 512)
         ).astype(BF)
         fc1.start()
+        r.sums[l, 1, 4:5, 0:512] = row_sum(r.pre[...].reshape(SEQ, 512).astype(F32))
 
         @pl.when(l == 0)
         def _():
@@ -725,12 +809,14 @@
             r.turned[part] = keys.astype(F32).T.astype(BF)
         r.dk[...] = jnp.zeros((SEQ, 128), F32)
         r.dv[...] = jnp.zeros((SEQ, 128), F32)
-        for who in (OWN, LEFT, RIGHT, FAR):
-            ring.arrive(who)
+
+        def attend(who):
             at = ring.at[who]
+            if who == FAR:
+                pl.when(l == 1)(self.ending_swap().start)
             r.gmix[at] = dot_nt(ring.rows(who), r.wout[l].reshape(2 * HD, D)).astype(BF)
 
-            def head_step(h, _, at=at):
+            def head_step(h, _):
                 queries, mine = r.q[l, at], r.gmix[at]
                 probs = jnp.exp(dot_nt(r.mk[h].reshape(SEQ, 128), queries) - r.lse[l, at, h])
                 back = dot_nt(r.mv[h].reshape(SEQ, 128), mine)
@@ -753,25 +839,22 @@
 
             lax.fori_loop(0, 2, head_step, 0)
             r.dq[at] = r.mixt[...].T.astype(BF)
+
+        ring.by_blocks(attend)
         for part in range(NX):
             span = slice(part * 2 * ROWS, (part + 1) * 2 * ROWS)
             r.dall[part] = jnp.concatenate(
                 [r.dq[part], r.dk[span, :].astype(BF), r.dv[span, :].astype(BF)], axis=1
             )
         weights = r.wqkv[l].reshape(3 * 2 * HD, D)
-        for who in (FAR, LEFT, RIGHT, OWN):
-            ring.put(who, dot_nn(r.dall[ring.at[who]], weights))
-            if who == LEFT:
-                ring.flush(FAR)
-            elif who == RIGHT:
-                ring.flush(LEFT)
-                ring.flush(RIGHT)
+        ring.back_by_blocks(lambda who: dot_nn(r.dall[ring.at[who]], weights))
         qkv, out = self.head_sums(l)
         whole = r.dall[...].reshape(SEQ, 384)
         dqkv = dot_tn(whole, r.normed[l, 0].reshape(SEQ, D)).astype(BF)
         r.dqkv[...] = dqkv.reshape(3, NZ, HD, D)
         qkv.start()
-        ring.merge()
+        ring.merge(0)
+        ring.merge(1)
         dout = dot_tn(r.mixed[l].reshape(SEQ, 128), gath[...].reshape(SEQ, D)).astype(BF)
         r.dout[...] = dout.reshape(NZ, HD, D)
         out.start()
@@ -821,7 +904,11 @@
 
         for s in range(1, 2 * NX):
             copy(s).start()
-        self.g_unit[...] = unit.total()
+        units = unit.total()
+        self.g_shift[...] = units[4:6]
+        for l in range(2):
+            self.g_unit[l : l + 1, 0:128] = units[2 * l : 2 * l + 1]
+            self.g_unit[l : l + 1, 128:256] = units[2 * l + 1 : 2 * l + 2]
         self.finish_heads(0)
         total = r.vec_sum[...]
         for s in range(1, 2 * NX):
@@ -838,12 +925,13 @@
     outs = [
         jax.ShapeDtypeStruct((ROWS, D), BF),
         jax.ShapeDtypeStruct((ROWS, D), F32),
-        jax.ShapeDtypeStruct((2, 128, 3 * HD), F32),
+        jax.ShapeDtypeStruct((2, 3, HD, 128), F32),
         jax.ShapeDtypeStruct((2, HD, 128), F32),
         jax.ShapeDtypeStruct((2, 128, 256), F32),
         jax.ShapeDtypeStruct((2, 256, 128), F32),
         jax.ShapeDtypeStruct((16, 128), F32),
-        jax.ShapeDtypeStruct((8, 128), F32),
+        jax.ShapeDtypeStruct((2, 128), F32),
+        jax.ShapeDtypeStruct((2, 256), F32),
     ]
     whole = pl.BlockSpec(memory_space=pltpu.VMEM)
     return pl.pallas_call(
@@ -875,10 +963,10 @@
     layer_scale,
     out_bias,
 ):
-    out_tokens, grad_tokens, g_qkv, g_out, g_fc1, g_fc2, g_vec, g_unit = run_whole(
+    out_tokens, grad_tokens, g_qkv, g_out, g_fc1, g_fc2, g_vec, g_shift, g_unit = run_whole(
         tokens,
         cotangent,
-        w_qkv.reshape(2, 128, 3 * HD),
+        jnp.swapaxes(w_qkv[:, :, 0, :], 1, 2).reshape(2, 3, HD, 128),
         qv_bias.reshape(2, 128),
         w_out.reshape(2, HD, 128),
         w_fc1,
@@ -893,11 +981,11 @@
     return (
         out_tokens,
         grad_tokens,
-        g_qkv[:, :, None, :],
-        g_unit[4:6][:, None, :],
+        jnp.swapaxes(g_qkv.reshape(2, 3 * HD, 128), 1, 2)[:, :, None, :],
+        g_shift[:, None, :],
         g_out[:, None],
         g_fc1,
-        g_unit[0:4].reshape(2, 256),
+        g_unit,
         g_fc2,
         vec[0],
         vec[1],

time: 311 us -> 286 us (0.920); the launches traced: 307 us -> 286 us
  Pallas kernels: 294 us -> 277 us
  local copies, waits for them, and re-layouts: 12.2 us -> 8.01 us
    pallas_call x1, Pallas kernels: 294 us -> 277 us  [run_whole(): pl.pallas_call(whole_kernel, out_shape=outs, in_specs=[whole] * len(args)...]
    unnamed x15 -> x22, local copies, waits for them, and re-layouts: 8.32 us -> 6.66 us
where the time goes in v1:
time: 286 us
  Pallas kernels  277 us (97%)
  local copies, waits for them, and re-layouts  8.01 us (3%)
    pallas_call x1, Pallas kernels, run_whole(): pl.pallas_call(whole_kernel, out_shape=outs, in_specs=[whole] * len(args)...  277 us
    unnamed x22, local copies, waits for them, and re-layouts  6.66 us

profile of v1, /device:TPU:1, one launch (start us, length us, event | category | flops | bytes accessed | tf_op | source)
XLA Modules:
  0.0 286.0 jit_solution(10972646343069987814)
XLA Ops:
  0.6 277.3 %shard_map.211 = (bf16[128,1024]{1,0:T(8,128)(2,1)}, f32[128,1024]{1,0:T(8,128)}, f32[2,3,64,128]{3,2,1,0:T(8,128)}, f32[2,64,128]{2,1,0:T(8,128)}, f32[2,128,25...) custom-call(bf16[128,1024]{1,0:T(8,128)(2,1)} %flat_0_.1, ...), custom_call_target="tpu_custom_call" | custom-call | flops 24000000000 | bytes 8000000 | tf_op jit(solution)/shard_map/pallas_call | solution.py:937
  278.0 0.0 copy-start
  278.0 1.4 fusion
  279.3 1.7 copy.34
  281.0 0.0 copy-done
  281.0 0.0 copy-start.3
  281.0 0.8 copy.35
  281.8 0.3 copy-done.3
  282.1 0.0 copy-start.6
  282.1 0.0 copy-start.4
  282.1 0.0 copy-start.2
  282.1 0.7 copy.36
  282.8 0.0 copy-done.6
  282.8 0.6 copy.37
  283.4 0.0 copy-done.4
  283.4 0.6 copy.38
  284.0 0.0 copy-done.2
  284.0 0.0 copy-start.5
  284.0 0.0 copy-start.1
  284.0 0.7 copy.39
  284.7 0.0 copy-done.5
  284.7 0.6 copy.40
  285.3 0.0 copy-done.1
  285.3 0.7 copy.41
Async XLA Ops:
  278.0 3.0 %copy-start = (f32[128,1024]{1,0:T(8,128)S(1)}, f32[128,1024]{1,0:T(8,128)}, u32[]{:S(2)}) copy-start(f32[128,1024]{1,0:T(8,128)} %get-tuple-element.59) | copy-start | bytes 1572868
  281.0 1.1 copy-start.3
  282.1 0.7 copy-start.6
  282.1 1.2 copy-start.4
  282.1 1.9 copy-start.2
  284.0 0.7 copy-start.5
  284.0 1.3 copy-start.1

commit v2 on v1

--- a/solution.py
+++ b/solution.py
@@ -28,7 +28,7 @@
 SCOPIES = 10
 TOP = pl.ds(0, HALF)
 BOTTOM = pl.ds(HALF, HALF)
-VMEM_BYTES = 60 * 1024 * 1024
+VMEM_BYTES = 62 * 1024 * 1024
 OWN, LEFT, RIGHT, FAR = 0, 1, 2, 3
 
 
@@ -124,6 +124,62 @@
     def wait(self):
         self.local().wait()
         each_peer(lambda s: self.copy(s).wait())
+
+
+class Relay:
+    def __init__(self, kind, src, dst, send, recv, y_first):
+        self.view, self.src, self.dst = VIEWS[kind], src, dst
+        self.send, self.recv, self.y_first = send, recv, y_first
+        f, z = group_index()
+        self.y, self.z = f // 2, z * 2 + lax.rem(f, 2)
+
+    def place(self, first, second):
+        y, z = (first, second) if self.y_first else (second, first)
+        y, z = lax.rem(self.y + y, 4), lax.rem(self.z + z, 4)
+        return y * 2 + lax.rem(z, 2), z // 2
+
+    def copy(self, first, second):
+        if second:
+            f, z = self.place(0, second)
+            origin = self.place(4 - first if first else 0, 0)
+        else:
+            f, z = self.place(first, 0)
+            origin = self.place(0, 0)
+        there = self.view(self.dst, *origin)
+        return pltpu.make_async_remote_copy(
+            src_ref=there if first and second else self.src,
+            dst_ref=there,
+            send_sem=self.send.at[first * 4 + second],
+            recv_sem=self.recv.at[first * 4 + second],
+            device_id={"fsdp": f, "tensor_1": z},
+            device_id_type=MESH,
+        )
+
+    def local(self):
+        return pltpu.make_async_copy(
+            self.src, self.view(self.dst, *self.place(0, 0)), self.send.at[0]
+        )
+
+    def start(self):
+        self.local().start()
+        for step in (2, 1, 3):
+            self.copy(step, 0).start()
+        for step in (2, 1, 3):
+            self.copy(0, step).start()
+
+    def pump(self):
+        for first in (1, 3, 2):
+            self.copy(first, 0).wait_recv()
+            for second in (2, 1, 3):
+                self.copy(first, second).start()
+
+    def wait(self):
+        self.local().wait()
+        for first in range(1, 4):
+            self.copy(first, 0).wait_send()
+        for first in range(4):
+            for second in range(1, 4):
+                self.copy(first, second).wait()
 
 
 class Scatter:
@@ -481,10 +537,10 @@
     dv=pltpu.VMEM((SEQ, 128), F32),
     dall=pltpu.VMEM((NX, 2 * ROWS, 384), BF),
     sums=pltpu.VMEM((2, 2, 8, D), F32),
-    dqkv=pltpu.VMEM((3, NZ, HD, D), BF),
-    dout=pltpu.VMEM((NZ, HD, D), BF),
-    dfc1=pltpu.VMEM((D, 512), BF),
-    dfc2=pltpu.VMEM((512, D), BF),
+    dqkv=pltpu.VMEM((2, 3, NZ, HD, D), BF),
+    dout=pltpu.VMEM((2, NZ, HD, D), BF),
+    dfc1=pltpu.VMEM((2, D, 512), BF),
+    dfc2=pltpu.VMEM((2, 512, D), BF),
     vec_src=pltpu.VMEM((16, D), F32),
     unit_src=pltpu.VMEM((NZ, 8, 128), F32),
     vec_sum=pltpu.VMEM((16, 128), F32),
@@ -559,22 +615,22 @@
     def unit_jobs(self, l):
         r = self.r
         return (
-            Gather("fc1", self.w_fc1.at[l], r.wfc1.at[l], *pair(r.fc1_sems, l)),
-            Gather("fc2", self.w_fc2.at[l], r.wfc2.at[l], *pair(r.fc2_sems, l)),
+            Relay("fc1", self.w_fc1.at[l], r.wfc1.at[l], *pair(r.fc1_sems, l), True),
+            Relay("fc2", self.w_fc2.at[l], r.wfc2.at[l], *pair(r.fc2_sems, l), False),
         )
 
     def head_sums(self, l):
         r = self.r
         return (
-            Scatter("qkv", r.dqkv, r.land_qkv.at[l], *pair(r.dqkv_sems, l)),
-            Scatter("out", r.dout, r.land_out.at[l], *pair(r.dout_sems, l)),
+            Scatter("qkv", r.dqkv.at[l], r.land_qkv.at[l], *pair(r.dqkv_sems, l)),
+            Scatter("out", r.dout.at[l], r.land_out.at[l], *pair(r.dout_sems, l)),
         )
 
     def unit_sums(self, l):
         r = self.r
         return (
-            Scatter("fc1", r.dfc1, r.land_fc1.at[l], *pair(r.dfc1_sems, l)),
-            Scatter("fc2", r.dfc2, r.land_fc2.at[l], *pair(r.dfc2_sems, l)),
+            Scatter("fc1", r.dfc1.at[l], r.land_fc1.at[l], *pair(r.dfc1_sems, l)),
+            Scatter("fc2", r.dfc2.at[l], r.land_fc2.at[l], *pair(r.dfc2_sems, l)),
         )
 
     def finish_heads(self, l):
@@ -605,8 +661,8 @@
             r.small_src[l, 11:16, :] = jnp.zeros((5, 128), F32)
         greeted()
         tokens = self.swap(0, self.tokens, r.start)
+        tokens.start()
         self.small_job().start()
-        tokens.start()
         for job in self.head_jobs(0):
             job.start()
         tokens.wait()
@@ -676,6 +732,8 @@
             r.turned[at] = values.astype(F32).T.astype(BF)
 
         ring.by_blocks(project)
+        for job in self.unit_jobs(l):
+            job.pump()
         pl.when(l == 0)(self.cotangent_swap().start)
 
         def attend(who):
@@ -779,20 +837,16 @@
 
         ring.by_chunks(step)
         fc1, fc2 = self.unit_sums(l)
-        r.dfc2[...] = dot_tn(
+        r.dfc2[l] = dot_tn(
             r.hidden[l].reshape(SEQ, 512), gath[...].reshape(SEQ, D)
         ).astype(BF)
         fc2.start()
         ring.merge(1)
-        r.dfc1[...] = dot_tn(
+        r.dfc1[l] = dot_tn(
             r.normed[l, 1].reshape(SEQ, D), r.pre[...].reshape(SEQ, 512)
         ).astype(BF)
         fc1.start()
         r.sums[l, 1, 4:5, 0:512] = row_sum(r.pre[...].reshape(SEQ, 512).astype(F32))
-
-        @pl.when(l == 0)
-        def _():
-            self.finish_heads(1)
 
         self.end_backward(l, 1, r.mid[l])
 
@@ -851,12 +905,12 @@
         qkv, out = self.head_sums(l)
         whole = r.dall[...].reshape(SEQ, 384)
         dqkv = dot_tn(whole, r.normed[l, 0].reshape(SEQ, D)).astype(BF)
-        r.dqkv[...] = dqkv.reshape(3, NZ, HD, D)
+        r.dqkv[l] = dqkv.reshape(3, NZ, HD, D)
         qkv.start()
         ring.merge(0)
         ring.merge(1)
         dout = dot_tn(r.mixed[l].reshape(SEQ, 128), gath[...].reshape(SEQ, D)).astype(BF)
-        r.dout[...] = dout.reshape(NZ, HD, D)
+        r.dout[l] = dout.reshape(NZ, HD, D)
         out.start()
         unit = row_sum(whole.astype(F32))
         r.sums[l, 0, 4:5, 0:256] = jnp.concatenate(
@@ -868,7 +922,6 @@
             ],
             axis=1,
         )
-        self.finish_units(l)
         self.end_backward(l, 0, r.stream[l])
 
     def last_sums(self):
@@ -890,6 +943,8 @@
         unit = Scatter("unit", r.unit_src, r.land_unit, *r.unit_sems)
         vec.start()
         unit.start()
+        self.finish_units(1)
+        self.finish_heads(1)
         r.vec_sum[...] = vec.total()
 
         def copy(step):
@@ -904,6 +959,7 @@
 
         for s in range(1, 2 * NX):
             copy(s).start()
+        self.finish_units(0)
         units = unit.total()
         self.g_shift[...] = units[4:6]
         for l in range(2):

time: 286 us -> 281 us (0.983)
  Pallas kernels: 277 us -> 272 us
    pallas_call x1, Pallas kernels: 277 us -> 272 us  [run_whole(): pl.pallas_call(whole_kernel, out_shape=outs, in_specs=[whole] * len(args)...]
where the time goes in v2:
time: 281 us
  Pallas kernels  272 us (97%)
  local copies, waits for them, and re-layouts  8.01 us (3%)
    pallas_call x1, Pallas kernels, run_whole(): pl.pallas_call(whole_kernel, out_shape=outs, in_specs=[whole] * len(args)...  272 us
    unnamed x22, local copies, waits for them, and re-layouts  6.66 us

profile of v2, /device:TPU:1, one launch (start us, length us, event | category | flops | bytes accessed | tf_op | source)
XLA Modules:
  0.0 281.0 jit_solution(10068908934108603850)
XLA Ops:
  0.6 272.3 %shard_map.211 = (bf16[128,1024]{1,0:T(8,128)(2,1)}, f32[128,1024]{1,0:T(8,128)}, f32[2,3,64,128]{3,2,1,0:T(8,128)}, f32[2,64,128]{2,1,0:T(8,128)}, f32[2,128,25...) custom-call(bf16[128,1024]{1,0:T(8,128)(2,1)} %flat_0_.1, ...), custom_call_target="tpu_custom_call" | custom-call | flops 24000000000 | bytes 8000000 | tf_op jit(solution)/shard_map/pallas_call | solution.py:993
  272.9 0.0 copy-start
  273.0 1.4 fusion
  274.3 1.7 copy.34
  276.0 0.0 copy-done
  276.0 0.0 copy-start.3
  276.0 0.8 copy.35
  276.8 0.3 copy-done.3
  277.1 0.0 copy-start.6
  277.1 0.0 copy-start.4
  277.1 0.0 copy-start.2
  277.1 0.7 copy.36
  277.8 0.0 copy-done.6
  277.8 0.6 copy.37
  278.4 0.0 copy-done.4
  278.4 0.6 copy.38
  279.0 0.0 copy-done.2
  279.0 0.0 copy-start.5
  279.0 0.0 copy-start.1
  279.0 0.7 copy.39
  279.7 0.0 copy-done.5
  279.7 0.6 copy.40
  280.3 0.0 copy-done.1
  280.3 0.7 copy.41
Async XLA Ops:
  272.9 3.0 %copy-start = (f32[128,1024]{1,0:T(8,128)S(1)}, f32[128,1024]{1,0:T(8,128)}, u32[]{:S(2)}) copy-start(f32[128,1024]{1,0:T(8,128)} %get-tuple-element.59) | copy-start | bytes 1572868
  276.0 1.1 copy-start.3
  277.1 0.7 copy-start.6
  277.1 1.2 copy-start.4
  277.1 1.9 copy-start.2
  279.0 0.7 copy-start.5
  279.0 1.3 copy-start.1

commit v3 on v2

--- a/solution.py
+++ b/solution.py
@@ -310,10 +310,16 @@
             self.go(ch, 1, 3, 2, 4, 0)
 
     def near(self, ch):
+        self.relay(ch)
+        self.pass_on(ch)
+
+    def relay(self, ch):
         self.got(ch, 1)
         self.go(ch, 5)
         self.got(ch, 3)
         self.go(ch, 6)
+
+    def pass_on(self, ch):
         self.got(ch, 2)
         self.go(ch, 7)
         self.got(ch, 4)
@@ -397,6 +403,9 @@
         self.send(ch, 5, self.held[ch, 1] + self.rin[ch, 1].astype(F32))
 
     def finish(self):
+        for ch in range(CHUNKS):
+            for i in range(GCOPIES):
+                self.gcopy(ch, i).wait_send()
         rows = []
         for ch in range(CHUNKS):
             total = self.both_cores(ch, OWN)
@@ -408,8 +417,6 @@
 
     def drain(self):
         for ch in range(CHUNKS):
-            for i in range(GCOPIES):
-                self.gcopy(ch, i).wait_send()
             for i in range(6):
                 self.scopy(ch, i).wait_send()
             for i in range(4):
@@ -457,6 +464,23 @@
         self.arrive_both(FAR)
         step(FAR)
 
+    def by_pairs(self, step):
+        self.arrive_both(OWN)
+        step((OWN, 0), (OWN, 1))
+        self.near(0)
+        self.relay(1)
+        self.arrive(0, LEFT)
+        self.arrive(0, RIGHT)
+        step((LEFT, 0), (RIGHT, 0))
+        self.pass_on(1)
+        self.far(0)
+        self.far(1)
+        self.arrive(1, LEFT)
+        self.arrive(1, RIGHT)
+        step((LEFT, 1), (RIGHT, 1))
+        self.arrive_both(FAR)
+        step((FAR, 0), (FAR, 1))
+
     def back_by_blocks(self, value):
         for who in (FAR, LEFT, RIGHT, OWN):
             self.put_both(who, value(who))
@@ -481,6 +505,10 @@
 
 def lane_head(shape):
     return lax.broadcasted_iota(jnp.int32, shape, len(shape) - 1) // HD
+
+
+def span_of(half):
+    return slice(half * 2 * PART, (half + 1) * 2 * PART)
 
 
 def row_sum(value):
@@ -531,7 +559,9 @@
     mixt=pltpu.VMEM((128, 2 * ROWS), F32),
     gath=pltpu.VMEM((2, NX, CHUNKS, 2, PART, D), BF),
     pre=pltpu.VMEM((NX, 2 * ROWS, 512), BF),
-    gmix=pltpu.VMEM(HEADS, BF),
+    gmix=pltpu.VMEM((2 * ROWS, 128), BF),
+    qmix=pltpu.VMEM((2 * ROWS, 128), BF),
+    lmix=pltpu.VMEM((2, 1, 2 * ROWS), F32),
     dq=pltpu.VMEM(HEADS, BF),
     dk=pltpu.VMEM((SEQ, 128), F32),
     dv=pltpu.VMEM((SEQ, 128), F32),
@@ -676,6 +706,7 @@
         r.start[...] = r.grad[...].astype(BF)
         back = self.swap(3, r.start, r.back)
         back.start()
+        self.ring.drain()
         self.last_sums()
         self.ending_swap().wait()
         back.wait()
@@ -702,6 +733,7 @@
         vec = r.small[0, l]
         normal, _ = norm_parts(r.stream[l])
         ring.set_own(r.normed.at[l, 0], (normal * vec[0:1] + vec[2:3]).astype(BF))
+        pl.when(l > 0)(ring.drain)
         bias_a, bias_b = r.small[0, l][10:11, 0:128], r.small[1, l][10:11, 0:128]
         shift = jnp.concatenate(
             [
@@ -767,13 +799,13 @@
         branch = ring.finish() + vec[6:7]
         r.branch[l, 0] = branch
         r.mid[l] = r.stream[l] + vec[4:5] * branch
-        ring.drain()
 
     def mlp_forward(self, l):
         r, ring = self.r, self.ring
         vec = r.small[0, l]
         normal, _ = norm_parts(r.mid[l])
         ring.set_own(r.normed.at[l, 1], (normal * vec[1:2] + vec[3:4]).astype(BF))
+        ring.drain()
         bias = jnp.concatenate(
             [r.small[z, l][row : row + 1, 0:128] for z in range(NZ) for row in (8, 9)], axis=1
         )
@@ -801,13 +833,13 @@
         branch = ring.finish() + vec[7:8]
         r.branch[l, 1] = branch
         r.stream[l + 1] = r.mid[l] + vec[5:6] * branch
-        ring.drain()
 
     def begin_backward(self, l, i, gath):
         r = self.r
         g = r.grad[...]
         scaled = r.small[0, l][4 + i : 5 + i] * g
         self.ring.set_own(gath, scaled.astype(BF))
+        self.ring.drain()
         r.sums[l, i] = jnp.zeros((8, D), F32)
         r.sums[l, i, 2:3, :] = row_sum(r.branch[l, i] * g)
         r.sums[l, i, 3:4, :] = row_sum(scaled)
@@ -820,7 +852,6 @@
         r.sums[l, i, 1:2, :] = row_sum(back)
         gain = r.small[0, l][i : i + 1]
         r.grad[...] += norm_backward(back, normal, inverse, gain)
-        self.ring.drain()
 
     def mlp_backward(self, l):
         r, ring = self.r, self.ring
@@ -864,15 +895,23 @@
         r.dk[...] = jnp.zeros((SEQ, 128), F32)
         r.dv[...] = jnp.zeros((SEQ, 128), F32)
 
-        def attend(who):
-            at = ring.at[who]
-            if who == FAR:
+        def attend(*halves):
+            if halves[0][0] == FAR:
                 pl.when(l == 1)(self.ending_swap().start)
-            r.gmix[at] = dot_nt(ring.rows(who), r.wout[l].reshape(2 * HD, D)).astype(BF)
+            at = [ring.at[who] for who, _ in halves]
+            span = [slice(ch * 2 * PART, (ch + 1) * 2 * PART) for _, ch in halves]
+            rows = jnp.concatenate([ring.chunk(ch, who) for who, ch in halves], axis=0)
+            r.gmix[...] = dot_nt(rows, r.wout[l].reshape(2 * HD, D)).astype(BF)
+            for i in range(2):
+                r.qmix[span_of(i), :] = r.q[l, at[i], span[i], :]
+            for h in range(2):
+                r.lmix[h] = jnp.concatenate(
+                    [r.lse[l, at[i], h][:, span[i]] for i in range(2)], axis=1
+                )
 
             def head_step(h, _):
-                queries, mine = r.q[l, at], r.gmix[at]
-                probs = jnp.exp(dot_nt(r.mk[h].reshape(SEQ, 128), queries) - r.lse[l, at, h])
+                queries, mine = r.qmix[...], r.gmix[...]
+                probs = jnp.exp(dot_nt(r.mk[h].reshape(SEQ, 128), queries) - r.lmix[h])
                 back = dot_nt(r.mv[h].reshape(SEQ, 128), mine)
                 delta = jnp.sum(probs * back, axis=0, keepdims=True)
                 dscores = (probs * (back - delta)).astype(BF)
@@ -892,9 +931,11 @@
                 return 0
 
             lax.fori_loop(0, 2, head_step, 0)
-            r.dq[at] = r.mixt[...].T.astype(BF)
-
-        ring.by_blocks(attend)
+            turned = r.mixt[...].T.astype(BF)
+            for i in range(2):
+                r.dq[at[i], span[i], :] = turned[span_of(i)]
+
+        ring.by_pairs(attend)
         for part in range(NX):
             span = slice(part * 2 * ROWS, (part + 1) * 2 * ROWS)
             r.dall[part] = jnp.concatenate(

time: 281 us -> 279 us (level)
  no operation moved by 1% of the time
where the time goes in v3:
time: 279 us
  Pallas kernels  270 us (97%)
  local copies, waits for them, and re-layouts  8.01 us (3%)
    pallas_call x1, Pallas kernels, run_whole(): pl.pallas_call(whole_kernel, out_shape=outs, in_specs=[whole] * len(args)...  270 us
    unnamed x22, local copies, waits for them, and re-layouts  6.66 us

profile of v3, /device:TPU:1, one launch (start us, length us, event | category | flops | bytes accessed | tf_op | source)
XLA Modules:
  0.0 279.1 jit_solution(13937697692486671248)
XLA Ops:
  0.6 270.4 %shard_map.211 = (bf16[128,1024]{1,0:T(8,128)(2,1)}, f32[128,1024]{1,0:T(8,128)}, f32[2,3,64,128]{3,2,1,0:T(8,128)}, f32[2,64,128]{2,1,0:T(8,128)}, f32[2,128,25...) custom-call(bf16[128,1024]{1,0:T(8,128)(2,1)} %flat_0_.1, ...), custom_call_target="tpu_custom_call" | custom-call | flops 24000000000 | bytes 8000000 | tf_op jit(solution)/shard_map/pallas_call | solution.py:1034
  271.0 0.0 copy-start
  271.0 1.4 fusion
  272.4 1.7 copy.34
  274.1 0.0 copy-done
  274.1 0.0 copy-start.3
  274.1 0.8 copy.35
  274.9 0.3 copy-done.3
  275.2 0.0 copy-start.6
  275.2 0.0 copy-start.4
  275.2 0.0 copy-start.2
  275.2 0.7 copy.36
  275.9 0.0 copy-done.6
  275.9 0.6 copy.37
  276.4 0.0 copy-done.4
  276.4 0.6 copy.38
  277.1 0.0 copy-done.2
  277.1 0.0 copy-start.5
  277.1 0.0 copy-start.1
  277.1 0.7 copy.39
  277.8 0.0 copy-done.5
  277.8 0.6 copy.40
  278.4 0.0 copy-done.1
  278.4 0.7 copy.41
Async XLA Ops:
  271.0 3.0 %copy-start = (f32[128,1024]{1,0:T(8,128)S(1)}, f32[128,1024]{1,0:T(8,128)}, u32[]{:S(2)}) copy-start(f32[128,1024]{1,0:T(8,128)} %get-tuple-element.59) | copy-start | bytes 1572868
  274.1 1.1 copy-start.3
  275.2 0.7 copy-start.6
  275.2 1.2 copy-start.4
  275.2 1.9 copy-start.2
  277.1 0.7 copy-start.5
  277.1 1.3 copy-start.1
